TPU v7x, 32 devices: a whole 2x2x4 slice. The times are simulated.
32 devices in a mesh: dp: 4 (over z), code: 8 (over y, x, core).
Axes of the slice: x: 2, y: 2, z: 4, core: 2. Of those that a mesh axis runs over, the one named last changes fastest.
Arguments:
- residuals: bfloat16 [8192, 1024], P('dp'), may hold values from -6 to 6
- codes: int32 [8192, 128], P('dp', 'code'), may hold values from 0 to 255, as said below
- codebook: float32 [128, 256, 8], P('code'), may hold values from -6 to 6
Outputs:
- rotated: float32 [8192, 1024], P('dp', 'code')
- new_codebook: float32 [128, 256, 8], P('code')
Inputs may be any that keep to these rules, and one draw needn't show every extreme that they name: `codes`: each entry names a codeword of its subspace.
All inputs are finite; a program needn't handle non-finite values.
Results may differ from a plain program's by a relative error of at most 0.008.
Values may be sent and summed in bfloat16 or wider, within the bound.
No kernel may reach another device: no remote copies, remote signals or barrier semaphores. Data moves between devices by JAX's collectives and lax.ppermute only.
A program may use at most 64 MiB of HBM per device.

v0:
```python
import functools

import jax
import jax.numpy as jnp
from jax import lax
from jax.experimental import pallas as pl
from jax.experimental.pallas import tpu as pltpu
from jax.sharding import PartitionSpec as P

quintic_a = 3.4445
quintic_b = -4.775
quintic_c = 2.0315
prior_weight = 8.0
epsilon = 1e-06
f32, bf16 = jnp.float32, jnp.bfloat16
MIB = 1024 * 1024
NT = (((1,), (1,)), ((), ()))


def dot(left, right):
    return jnp.dot(left, right, preferred_element_type=f32)


def dot_nt(left, right):
    return lax.dot_general(left, right, NT, preferred_element_type=f32)


def cross_kernel(codes_hbm, book_hbm, res_hbm, *refs, dp):
    outs = refs[: dp or 1]
    codes_ref, book_ref, res_ref, recon, cross, sems = refs[dp or 1 :]
    loads = [
        pltpu.make_async_copy(codes_hbm, codes_ref, sems.at[0]),
        pltpu.make_async_copy(book_hbm, book_ref, sems.at[1]),
        pltpu.make_async_copy(res_hbm, res_ref, sems.at[2]),
    ]
    for load in loads:
        load.start()
    loads[0].wait()
    loads[1].wait()
    subs, rows = codes_ref.shape
    width = book_ref.shape[0] // subs
    words = book_ref.shape[1]
    lanes = 128
    for m in range(subs):
        band = pl.ds(m * width, width)
        tables = [book_ref[band, pl.ds(t * lanes, lanes)] for t in range(words // lanes)]
        for c in range(rows // lanes):
            cols = pl.ds(c * lanes, lanes)
            code = jnp.broadcast_to(codes_ref[pl.ds(m, 1), cols], (width, lanes))
            low = jnp.bitwise_and(code, lanes - 1)
            value = jnp.take_along_axis(tables[0], low, axis=1, mode="promise_in_bounds")
            for t in range(1, len(tables)):
                other = jnp.take_along_axis(tables[t], low, axis=1, mode="promise_in_bounds")
                value = jnp.where(code >= t * lanes, other, value)
            recon[band, cols] = value
    loads[2].wait()
    if dp is None:
        outs[0][...] = dot(recon[...].astype(bf16), res_ref[...])
        return
    cross[...] = dot(recon[...].astype(bf16), res_ref[...])
    place = lax.axis_index("dp")
    size = outs[0].shape[0]
    for k, out in enumerate(outs):
        at = pl.multiple_of(jnp.bitwise_xor(place, k) * size, size)
        out[...] = cross[pl.ds(at, size), :].astype(out.dtype)


def cross_partial(codes_t, book_t, residuals, dp):
    rows, dim = residuals.shape
    cols = book_t.shape[0]
    if dp is None:
        shapes = (jax.ShapeDtypeStruct((cols, dim), f32),)
    else:
        shapes = tuple(
            jax.ShapeDtypeStruct((cols // dp, dim), bf16 if k else f32) for k in range(dp)
        )
    shapes += tuple(jax.ShapeDtypeStruct(x.shape, x.dtype) for x in (codes_t, book_t, residuals))
    return pl.pallas_call(
        functools.partial(cross_kernel, dp=dp),
        out_shape=shapes,
        in_specs=[pl.BlockSpec(memory_space=pltpu.HBM)] * 3,
        out_specs=(pl.BlockSpec(memory_space=pltpu.VMEM),) * len(shapes),
        scratch_shapes=[
            pltpu.VMEM((cols, rows), f32),
            pltpu.VMEM((cols, dim), f32),
            pltpu.SemaphoreType.DMA((3,)),
        ],
        compiler_params=pltpu.CompilerParams(vmem_limit_bytes=24 * MIB),
        name="cross_partial",
    )(*[pltpu.with_memory_space_constraint(x, pltpu.HBM) for x in (codes_t, book_t, residuals)])


def polar_kernel(*refs, blocks, pieces, chunk):
    block_refs = refs[:blocks]
    rot_b = refs[blocks]
    raw, gram, gram_b, poly_b, iterate, iterate_b = refs[blocks + 1 :]
    dim = raw.shape[0]
    own = rot_b.shape[0]
    steps = dim // chunk
    at = 0
    for block in block_refs:
        raw[pl.ds(at, block.shape[0]), :] = block[...]
        at += block.shape[0]

    def band_of(i):
        return pl.ds(i * chunk, chunk)

    def lower(j):
        return pl.ds(j * chunk, dim - j * chunk), pl.ds(j * chunk, chunk)

    def mirror(target, j, value):
        rows, cols = lower(j)
        target[rows, cols] = value.astype(bf16)
        for i in range(j + 1, steps):
            at = (i - j) * chunk
            target[cols, pl.ds(i * chunk, chunk)] = value[at : at + chunk, :].T.astype(bf16)

    def gram_of(source):
        r = lax.broadcasted_iota(jnp.int32, (chunk, chunk), 0)
        c = lax.broadcasted_iota(jnp.int32, (chunk, chunk), 1)
        trace = jnp.zeros((), f32)
        for j in range(steps):
            rows, cols = lower(j)
            part = dot_nt(source[rows, :], source[cols, :])
            gram[rows, cols] = part
            mirror(gram_b, j, part)
            trace = trace + jnp.sum(jnp.where(r == c, part[:chunk, :], 0.0))
        return trace

    def poly_of(wb, wc):
        for j in range(steps):
            rows, cols = lower(j)
            square = dot(gram_b[rows, :], gram_b[:, cols])
            mirror(poly_b, j, wb * gram[rows, cols] + wc * square)

    frob = gram_of(raw)
    scale2 = 1.0 / (frob + epsilon)
    scale = lax.rsqrt(frob + epsilon)
    poly_of(quintic_b * scale2, quintic_c * scale2 * scale2)

    for i in range(steps):
        cols = band_of(i)
        value = scale * (quintic_a * raw[:, cols].astype(f32) + dot(poly_b[...], raw[:, cols]))
        iterate[:, cols] = value
        iterate_b[:, cols] = value.astype(bf16)

    gram_of(iterate_b)
    poly_of(quintic_b, quintic_c)

    for i in range(steps):
        cols = band_of(i)
        value = quintic_a * iterate[:, cols] + dot(poly_b[...], iterate_b[:, cols])
        iterate[:, cols] = value
        raw[:, cols] = value.astype(bf16)

    mine = pl.ds(0, own)
    g = dot_nt(raw[mine, :], raw[...])
    image = dot(g.astype(bf16), raw[...])
    square = dot_nt(image.astype(bf16), raw[...])
    last = quintic_a * iterate[mine, :] + dot(
        (quintic_b * g + quintic_c * square).astype(bf16), raw[...]
    )
    size = own // pieces
    for p in range(pieces):
        to = 0
        if pieces > 1:
            to = pl.multiple_of(jnp.bitwise_xor(lax.axis_index("dp"), p) * size, size)
        rot_b[pl.ds(to, size), :] = last[p * size : (p + 1) * size, :].astype(bf16)


LOWS = 64


def onehot_kernel(codes_ref, onehot_ref, counts_ref):
    subs, rows_all = codes_ref.shape
    highs = counts_ref.shape[1] // LOWS
    low_word = lax.broadcasted_iota(jnp.int32, (LOWS, rows_all), 0)
    high_word = lax.broadcasted_iota(jnp.int32, (8, rows_all), 0)
    for m in range(subs):
        code = codes_ref[pl.ds(m, 1), :]
        low, high = jnp.bitwise_and(code, LOWS - 1), jnp.right_shift(code, 6)
        onehot = jnp.where(low_word == low, 1.0, 0.0).astype(bf16)
        onehot_ref[pl.ds(m * LOWS, LOWS), :] = onehot
        part = dot_nt(jnp.where(high_word == high, 1.0, 0.0).astype(bf16), onehot)
        for h in range(highs):
            counts_ref[pl.ds(m, 1), pl.ds(h * LOWS, LOWS)] = part[h : h + 1, :]


def onehot_call(codes_t, words):
    subs, rows = codes_t.shape
    vmem = pl.BlockSpec(memory_space=pltpu.VMEM)
    return pl.pallas_call(
        onehot_kernel,
        out_shape=(
            jax.ShapeDtypeStruct((subs * LOWS, rows), bf16),
            jax.ShapeDtypeStruct((subs, words), f32),
        ),
        in_specs=[vmem],
        out_specs=(vmem, vmem),
        compiler_params=pltpu.CompilerParams(vmem_limit_bytes=24 * MIB),
        cost_estimate=pl.CostEstimate(
            flops=2 * 256 * subs * LOWS * rows, bytes_accessed=2 * subs * LOWS * rows, transcendentals=0
        ),
        name="onehot",
    )(codes_t)


def sums_kernel(rot_ref, res_ref, codes_ref, onehot_ref, counts_ref, sent_ref, sums_ref):
    subs, rows_all = codes_ref.shape
    own = rot_ref.shape[0]
    words = counts_ref.shape[1]
    width = own // subs
    highs = words // LOWS
    group = min(subs, 256 // LOWS)
    rot_t = dot_nt(rot_ref[...], res_ref[...])
    for first in range(0, subs, group):
        values = []
        for m in range(first, first + group):
            high = jnp.right_shift(codes_ref[pl.ds(m, 1), :], 6)
            band = rot_t[m * width : (m + 1) * width, :]
            values += [jnp.where(high == h, band, 0.0) for h in range(highs)]
        tall = jnp.concatenate(values, axis=0).astype(bf16)
        part = dot_nt(tall, onehot_ref[pl.ds(first * LOWS, group * LOWS), :])
        for s in range(group):
            for h in range(highs):
                at = (s * highs + h) * width
                sums_ref[pl.ds((first + s) * width, width), pl.ds(h * LOWS, LOWS)] = part[
                    at : at + width, s * LOWS : (s + 1) * LOWS
                ]
    sent_ref[pl.ds(0, own), :] = sums_ref[...].astype(bf16)
    sent_ref[pl.ds(own, subs), :] = counts_ref[...].astype(bf16)


def rotated_kernel(rot_ref, res_ref, rotated_ref):
    rows_all = res_ref.shape[0]
    step = 512

    @pl.loop(0, rows_all // step)
    def _(i):
        rows = pl.ds(pl.multiple_of(i * step, step), step)
        rotated_ref[rows, :] = dot_nt(res_ref[rows, :], rot_ref[...])


def polar(block_list, own, pieces):
    dim = block_list[0].shape[1]
    vmem = pl.BlockSpec(memory_space=pltpu.VMEM)
    kernel = functools.partial(polar_kernel, blocks=len(block_list), pieces=pieces, chunk=256)
    return pl.pallas_call(
        kernel,
        out_shape=jax.ShapeDtypeStruct((own, dim), bf16),
        in_specs=[vmem] * len(block_list),
        out_specs=vmem,
        scratch_shapes=[
            pltpu.VMEM((dim, dim), bf16),
            pltpu.VMEM((dim, dim), f32),
            pltpu.VMEM((dim, dim), bf16),
            pltpu.VMEM((dim, dim), bf16),
            pltpu.VMEM((dim, dim), f32),
            pltpu.VMEM((dim, dim), bf16),
        ],
        compiler_params=pltpu.CompilerParams(vmem_limit_bytes=36 * MIB),
        name="polar",
    )(*block_list)


def share_kernel(*refs):
    total = refs[0][...].astype(f32)
    for part in refs[1:-1]:
        total = total + part[...].astype(f32)
    refs[-1][...] = total.astype(refs[-1].dtype)


def book_kernel(book_ref, *refs):
    sums, out_ref = refs[:-1], refs[-1]
    own = book_ref.shape[0]
    subs = sums[0].shape[0] - own
    width = own // subs
    total = sums[0][...].astype(f32)
    for part in sums[1:]:
        total = total + part[...].astype(f32)
    for m in range(subs):
        band = pl.ds(m * width, width)
        count = total[own + m : own + m + 1, :] + prior_weight
        part = total[m * width : (m + 1) * width, :]
        out_ref[band, :] = (part + prior_weight * book_ref[band, :]) / count


def small_call(kernel, name, shape, dtype, *operands, scratch=()):
    vmem = pl.BlockSpec(memory_space=pltpu.VMEM)
    return pl.pallas_call(
        kernel,
        out_shape=jax.ShapeDtypeStruct(shape, dtype),
        in_specs=[vmem] * len(operands),
        out_specs=vmem,
        scratch_shapes=scratch,
        compiler_params=pltpu.CompilerParams(vmem_limit_bytes=24 * MIB),
        name=name,
    )(*operands)


def swap(value, axis, size, mask, odd_mask=None):
    odd_mask = mask if odd_mask is None else odd_mask
    return lax.ppermute(value, axis, [(i, i ^ (odd_mask if i % 2 else mask)) for i in range(size)])


def make_body(dp, code):
    def body(residuals, codes, codebook):
        rows, dim = residuals.shape
        subs, words, width = codebook.shape
        own = subs * width
        codes_t = codes.T
        book_t = jnp.transpose(codebook, (0, 2, 1)).reshape(own, words)
        size = own // dp
        thin = size % 16 != 0
        if thin:
            place = lax.axis_index("dp")
            partial, codes_v, book_v, res_v = cross_partial(codes_t, book_t, residuals, None)
            cut = [
                lax.dynamic_slice_in_dim(partial, (place ^ k) * size, size, 0) for k in range(dp)
            ]
            parts = [cut[0]] + [part.astype(bf16) for part in cut[1:]]
        else:
            *parts, codes_v, book_v, res_v = cross_partial(codes_t, book_t, residuals, dp)
        far_first = range(dp - 1, 0, -1)
        got = [swap(parts[k], "dp", dp, k) for k in far_first]
        onehot, counts = onehot_call(codes_v, words)
        *got, onehot, counts = lax.optimization_barrier((*got, onehot, counts))
        piece = small_call(share_kernel, "share", (size, dim), bf16, parts[0], *got)
        pieces = {0: piece}
        for k in far_first:
            pieces[k] = swap(piece, "dp", dp, k)
        if thin:
            block = jnp.zeros((own, dim), bf16)
            for k in range(dp):
                block = lax.dynamic_update_slice_in_dim(block, pieces[k], (place ^ k) * size, 0)
            held = [block]
        else:
            held = [piece]
            if dp > 1:
                held.append(jnp.concatenate([pieces[k] for k in range(1, dp)], axis=0))
        strides = [1 << b for b in reversed(range(code.bit_length() - 1))]
        far, near = strides[:-1], strides[-1:]

        def spread(blocks, beside=()):
            for even, odd in zip(far, far[::-1]):
                new = [swap(t, "code", code, even, odd) for t in blocks]
                if beside:
                    new, beside = lax.optimization_barrier((new, list(beside)))
                blocks = blocks + new
            return blocks, list(beside)

        def across(block):
            return [swap(block, "code", code, stride) for stride in near]

        if held[1:]:
            first, _ = spread(held[:1])
            known = 1 + len(first) // 2
            early, rest = lax.optimization_barrier((first[:known], held[1]))
            crossed = across(jnp.concatenate(early, axis=0)) + across(rest)
            blocks, beside = spread([rest], first[known:] + crossed)
            late, crossed = beside[: len(first) - known], beside[len(first) - known :]
            held = [early[0], rest] + early[1:] + late + blocks[1:] + crossed
            held += [t for block in late + blocks[1:] for t in across(block)]
        else:
            held, _ = spread(held)
            held += [t for block in held for t in across(block)]
        rotation_t = polar(held, own, 1 if thin else dp)
        scratch = [pltpu.VMEM((own, words), f32)]
        operands = (rotation_t, res_v, codes_v, onehot, counts)
        sums = small_call(sums_kernel, "sums", (own + subs, words), bf16, *operands, scratch=scratch)
        rotated = small_call(rotated_kernel, "rotated", (rows, own), f32, rotation_t, res_v)
        others = [swap(sums, "dp", dp, k) for k in far_first]
        book = small_call(book_kernel, "book", (own, words), f32, book_v, sums, *others)
        return rotated, jnp.transpose(book.reshape(subs, width, words), (0, 2, 1))

    return body


def solution(mesh):
    dp, code = mesh.shape["dp"], mesh.shape["code"]
    in_specs = (P("dp", None), P("dp", "code"), P("code", None, None))
    out_specs = (P("dp", "code"), P("code", None, None))
    return jax.shard_map(
        make_body(dp, code), mesh=mesh, in_specs=in_specs, out_specs=out_specs, check_vma=False
    )
```

profile of v0, /device:TPU:0, one launch (start us, length us, event | category | flops | bytes accessed | tf_op | source)
XLA Modules:
  0.0 65.7 jit_solution(2200462521076800467)
XLA Ops:
  0.6 3.1 %cross_partial.1 = (f32[32,1024]{1,0:T(8,128)S(1)}, bf16[32,1024]{1,0:T(8,128)(2,1)S(1)}, bf16[32,1024]{1,0:T(8,128)(2,1)S(1)}, bf16[32,1024]{1,0:T(8,128)(2,1)S...) custom-call(s32[16,2048]{1,0:T(8,128)} %bitcast.7, f32[128,256]{1,0:T(8,128)} %bitcast.8, ...), custom_call_target="tpu_custom_call" | custom-call | tf_op jit(solution)/shard_map/cross_partial/pallas_call | solution.py:78
  3.7 5.1 %collective-permute-start = (bf16[32,1024]{1,0:T(8,128)(2,1)S(1)}, bf16[32,1024]{1,0:T(8,128)(2,1)S(1)}, u32[]{:S(2)}, u32[]{:S(2)}) collective-permute-start(bf16[32,1024]{1,0:T(8,128)(2,1)S(1)} %get-tuple-element.30), channel_id=1, source_target_pairs={{0,24},{8,16},{16,8},{24,0},{1,25},{9,17},{17,9},{25,1},{2,26},{10... | collective-permute-start | bytes 196616 | tf_op jit(solution)/shard_map/ppermute | solution.py:303
  8.9 0.0 collective-permute-start.1
  8.9 0.6 collective-permute-start.2
  9.5 1.9 %onehot.1 = (bf16[1024,2048]{1,0:T(8,128)(2,1)S(1)}, f32[16,256]{1,0:T(8,128)S(1)}) custom-call(s32[16,2048]{1,0:T(8,128)S(1)} %get-tuple-element.33.codes_ref), custom_call_target="tpu_custom_call" | custom-call | flops 1073741824 | bytes 4194304 | tf_op jit(solution)/shard_map/onehot/pallas_call | solution.py:192
  11.4 0.0 collective-permute-done.refs_1_
  11.5 3.0 %collective-permute-done.1.refs_2_ = bf16[32,1024]{1,0:T(8,128)(2,1)S(1)} collective-permute-done((bf16[32,1024]{1,0:T(8,128)(2,1)S(1)}, bf16[32,1024]{1,0:T(8,128)(2,1)S(1)}, u32[]{:S(2)}, u32[]{:S(2)}) %collective-permute-start.1) | collective-permute-done | bytes 65568 | tf_op jit(solution)/shard_map/ppermute | solution.py:303
  14.5 0.0 collective-permute-done.2.refs_3_
  14.5 2.8 %collective-permute-start.7 = (bf16[32,1024]{1,0:T(8,128)(2,1)S(1)}, bf16[32,1024]{1,0:T(8,128)(2,1)S(1)}, u32[]{:S(2)}, u32[]{:S(2)}) collective-permute-start(bf16[32,1024]{1,0:T(8,128)(2,1)S(1)} %share.1.refs_0_), channel_id=1, source_target_pairs={{0,24},{8,16},{16,8},{24,0},{1,25},{9,17},{17,9},{25,1},{2,26},{10... | collective-permute-start | bytes 196616 | tf_op jit(solution)/shard_map/ppermute | solution.py:303
  17.3 0.0 collective-permute-start.6
  17.3 1.7 %collective-permute-start.5 = (bf16[32,1024]{1,0:T(8,128)(2,1)S(1)}, bf16[32,1024]{1,0:T(8,128)(2,1)S(1)}, u32[]{:S(2)}, u32[]{:S(2)}) collective-permute-start(bf16[32,1024]{1,0:T(8,128)(2,1)S(1)} %share.1.refs_0_), channel_id=1, source_target_pairs={{0,8},{8,0},{16,24},{24,16},{1,9},{9,1},{17,25},{25,17},{2,10},{10... | collective-permute-start | bytes 196616 | tf_op jit(solution)/shard_map/ppermute | solution.py:303
  19.0 1.5 %collective-permute-start.4 = (bf16[32,1024]{1,0:T(8,128)(2,1)S(1)}, bf16[32,1024]{1,0:T(8,128)(2,1)S(1)}, u32[]{:S(2)}, u32[]{:S(2)}) collective-permute-start(bf16[32,1024]{1,0:T(8,128)(2,1)S(1)} %share.1.refs_0_), channel_id=1, source_target_pairs={{0,2},{1,5},{2,0},{3,7},{4,6},{5,1},{6,4},{7,3},{8,10},{9,13},{10,... | collective-permute-start | bytes 196616 | tf_op jit(solution)/shard_map/ppermute | solution.py:303
  20.5 1.5 %collective-permute-start.3 = (bf16[32,1024]{1,0:T(8,128)(2,1)S(1)}, bf16[32,1024]{1,0:T(8,128)(2,1)S(1)}, u32[]{:S(2)}, u32[]{:S(2)}) collective-permute-start(bf16[32,1024]{1,0:T(8,128)(2,1)S(1)} %share.1.refs_0_), channel_id=1, source_target_pairs={{0,4},{1,3},{2,6},{3,1},{4,0},{5,7},{6,2},{7,5},{8,12},{9,11},{10,... | collective-permute-start | bytes 196616 | tf_op jit(solution)/shard_map/ppermute | solution.py:303
  22.0 0.0 collective-permute-done.7
  22.0 1.6 %collective-permute-done.6 = bf16[32,1024]{1,0:T(8,128)(2,1)S(1)} collective-permute-done((bf16[32,1024]{1,0:T(8,128)(2,1)S(1)}, bf16[32,1024]{1,0:T(8,128)(2,1)S(1)}, u32[]{:S(2)}, u32[]{:S(2)}) %collective-permute-start.6) | collective-permute-done | bytes 65568 | tf_op jit(solution)/shard_map/ppermute | solution.py:303
  23.6 0.0 collective-permute-done.5
  23.6 0.0 collective-permute-done.4.refs_3_
  23.6 1.1 %collective-permute-done.3.refs_2_ = bf16[32,1024]{1,0:T(8,128)(2,1)S(1)} collective-permute-done((bf16[32,1024]{1,0:T(8,128)(2,1)S(1)}, bf16[32,1024]{1,0:T(8,128)(2,1)S(1)}, u32[]{:S(2)}, u32[]{:S(2)}) %collective-permute-start.3) | collective-permute-done | bytes 65568 | tf_op jit(solution)/shard_map/ppermute | solution.py:303
  24.7 0.1 collective-permute-start.11
  24.8 0.5 collective-permute-start.12
  25.3 1.5 %collective-permute-start.9 = (bf16[96,1024]{1,0:T(8,128)(2,1)S(1)}, bf16[96,1024]{1,0:T(8,128)(2,1)S(1)}, u32[]{:S(2)}, u32[]{:S(2)}) collective-permute-start(bf16[96,1024]{1,0:T(8,128)(2,1)S(1)} %pad_maximum_fusion.refs_1_), channel_id=1, source_target_pairs={{0,4},{1,3},{2,6},{3,1},{4,0},{5,7},{6,2},{7,5},{8,12},{9,11},{10,... | collective-permute-start | bytes 589832 | tf_op jit(solution)/shard_map/ppermute | solution.py:303
  26.8 0.5 collective-permute-start.10
  27.4 1.5 %collective-permute-start.8 = (bf16[96,1024]{1,0:T(8,128)(2,1)S(1)}, bf16[96,1024]{1,0:T(8,128)(2,1)S(1)}, u32[]{:S(2)}, u32[]{:S(2)}) collective-permute-start(bf16[96,1024]{1,0:T(8,128)(2,1)S(1)} %pad_maximum_fusion.refs_1_), channel_id=1, source_target_pairs={{0,2},{1,5},{2,0},{3,7},{4,6},{5,1},{6,4},{7,3},{8,10},{9,13},{10,... | collective-permute-start | bytes 589832 | tf_op jit(solution)/shard_map/ppermute | solution.py:303
  28.9 2.2 %collective-permute-done.10.refs_4_ = bf16[32,1024]{1,0:T(8,128)(2,1)S(1)} collective-permute-done((bf16[32,1024]{1,0:T(8,128)(2,1)S(1)}, bf16[32,1024]{1,0:T(8,128)(2,1)S(1)}, u32[]{:S(2)}, u32[]{:S(2)}) %collective-permute-start.10) | collective-permute-done | bytes 65568 | tf_op jit(solution)/shard_map/ppermute | solution.py:303
  31.1 0.0 collective-permute-done.11.refs_8_
  31.1 0.0 collective-permute-done.12.refs_9_
  31.1 1.6 %collective-permute-done.9.refs_5_ = bf16[96,1024]{1,0:T(8,128)(2,1)S(1)} collective-permute-done((bf16[96,1024]{1,0:T(8,128)(2,1)S(1)}, bf16[96,1024]{1,0:T(8,128)(2,1)S(1)}, u32[]{:S(2)}, u32[]{:S(2)}) %collective-permute-start.9) | collective-permute-done | bytes 196640 | tf_op jit(solution)/shard_map/ppermute | solution.py:303
  32.7 0.6 collective-permute-start.13
  33.3 0.0 collective-permute-start.15
  33.3 0.0 collective-permute-done.8.refs_6_
  33.3 5.0 %collective-permute-done.13.refs_7_ = bf16[96,1024]{1,0:T(8,128)(2,1)S(1)} collective-permute-done((bf16[96,1024]{1,0:T(8,128)(2,1)S(1)}, bf16[96,1024]{1,0:T(8,128)(2,1)S(1)}, u32[]{:S(2)}, u32[]{:S(2)}) %collective-permute-start.13) | collective-permute-done | bytes 196640 | tf_op jit(solution)/shard_map/ppermute | solution.py:303
  38.4 0.0 collective-permute-start.16
  38.4 0.5 collective-permute-start.17
  38.9 0.0 collective-permute-start.14
  38.9 0.0 collective-permute-done.15.refs_11_
  38.9 1.3 %collective-permute-done.14.refs_10_ = bf16[32,1024]{1,0:T(8,128)(2,1)S(1)} collective-permute-done((bf16[32,1024]{1,0:T(8,128)(2,1)S(1)}, bf16[32,1024]{1,0:T(8,128)(2,1)S(1)}, u32[]{:S(2)}, u32[]{:S(2)}) %collective-permute-start.14) | collective-permute-done | bytes 65568 | tf_op jit(solution)/shard_map/ppermute | solution.py:303
  40.2 0.0 collective-permute-done.16.refs_12_
  40.2 0.0 collective-permute-done.17.refs_13_
  40.2 12.2 %polar.1.rot_ref = bf16[128,1024]{1,0:T(8,128)(2,1)S(1)} custom-call(bf16[32,1024]{1,0:T(8,128)(2,1)S(1)} %share.1.refs_0_, bf16[96,1024]{1,0:T(8,128)(2,1)S(1)} %pad_maximum_fusion.refs_1_, bf16[32,1024]{1,0:T(8,128)(2,1)S(1)} %collective-permute-done.3.refs_2_, bf16[32,1024]{1,0:T(8,128)(2,1)S(1)} %collective-permute-done.4.refs_3_, ...), custom_call_target="tpu_custom_call" | custom-call | tf_op jit(solution)/shard_map/polar/pallas_call | solution.py:248
  52.4 3.0 %sums.1.refs_0_ = bf16[144,256]{1,0:T(8,128)(2,1)S(1)} custom-call(bf16[128,1024]{1,0:T(8,128)(2,1)S(1)} %polar.1.rot_ref, bf16[2048,1024]{1,0:T(8,128)(2,1)S(1)} %get-tuple-element.52.res_ref, s32[16,2048]{1,0:T(8,128)S(1)} %get-tuple-element.33.codes_ref, bf16[1024,2048]{1,0:T(8,128)(2,1)S(1)} %get-tuple-element.54.onehot_ref, ...), custom_call_target="tpu_custom_call" | custom-call | tf_op jit(solution)/shard_map/sums/pallas_call | solution.py:290
  55.3 0.4 collective-permute-start.20
  55.8 2.9 %collective-permute-start.19 = (bf16[144,256]{1,0:T(8,128)(2,1)S(1)}, bf16[144,256]{1,0:T(8,128)(2,1)S(1)}, u32[]{:S(2)}, u32[]{:S(2)}) collective-permute-start(bf16[144,256]{1,0:T(8,128)(2,1)S(1)} %sums.1.refs_0_), channel_id=1, source_target_pairs={{0,16},{8,24},{16,0},{24,8},{1,17},{9,25},{17,1},{25,9},{2,18},{10... | collective-permute-start | bytes 221192 | tf_op jit(solution)/shard_map/ppermute | solution.py:303
  58.7 1.1 %collective-permute-start.18 = (bf16[144,256]{1,0:T(8,128)(2,1)S(1)}, bf16[144,256]{1,0:T(8,128)(2,1)S(1)}, u32[]{:S(2)}, u32[]{:S(2)}) collective-permute-start(bf16[144,256]{1,0:T(8,128)(2,1)S(1)} %sums.1.refs_0_), channel_id=1, source_target_pairs={{0,24},{8,16},{16,8},{24,0},{1,25},{9,17},{17,9},{25,1},{2,26},{10... | collective-permute-start | bytes 221192 | tf_op jit(solution)/shard_map/ppermute | solution.py:303
  59.8 2.7 %rotated.1 = f32[2048,128]{1,0:T(8,128)} custom-call(bf16[128,1024]{1,0:T(8,128)(2,1)S(1)} %polar.1.rot_ref, bf16[2048,1024]{1,0:T(8,128)(2,1)S(1)} %get-tuple-element.52.res_ref), custom_call_target="tpu_custom_call" | custom-call | tf_op jit(solution)/shard_map/rotated/pallas_call | solution.py:290
  62.5 0.0 collective-permute-done.20.refs_3_
  62.5 1.4 %collective-permute-done.19.refs_2_ = bf16[144,256]{1,0:T(8,128)(2,1)S(1)} collective-permute-done((bf16[144,256]{1,0:T(8,128)(2,1)S(1)}, bf16[144,256]{1,0:T(8,128)(2,1)S(1)}, u32[]{:S(2)}, u32[]{:S(2)}) %collective-permute-start.19) | collective-permute-done | bytes 73760 | tf_op jit(solution)/shard_map/ppermute | solution.py:303
  63.9 1.0 %collective-permute-done.18.refs_1_ = bf16[144,256]{1,0:T(8,128)(2,1)S(1)} collective-permute-done((bf16[144,256]{1,0:T(8,128)(2,1)S(1)}, bf16[144,256]{1,0:T(8,128)(2,1)S(1)}, u32[]{:S(2)}, u32[]{:S(2)}) %collective-permute-start.18) | collective-permute-done | bytes 73760 | tf_op jit(solution)/shard_map/ppermute | solution.py:303
  64.9 0.7 %book.1 = f32[128,256]{1,0:T(8,128)} custom-call(f32[128,256]{1,0:T(8,128)S(1)} %get-tuple-element.53.book_ref, bf16[144,256]{1,0:T(8,128)(2,1)S(1)} %sums.1.refs_0_, bf16[144,256]{1,0:T(8,128)(2,1)S(1)} %collective-permute-done.18.refs_1_, bf16[144,256]{1,0:T(8,128)(2,1)S(1)} %collective-permute-done.19.refs_2_, ...), custom_call_target="tpu_custom_call" | custom-call | tf_op jit(solution)/shard_map/book/pallas_call | solution.py:290
  (3 shorter events, 0.1 us)
Async XLA Ops:
  3.7 7.7 %collective-permute-start = (bf16[32,1024]{1,0:T(8,128)(2,1)S(1)}, bf16[32,1024]{1,0:T(8,128)(2,1)S(1)}, u32[]{:S(2)}, u32[]{:S(2)}) collective-permute-start(bf16[32,1024]{1,0:T(8,128)(2,1)S(1)} %get-tuple-element.30), channel_id=1, source_target_pairs={{0,24},{8,16},{16,8},{24,0},{1,25},{9,17},{17,9},{25,1},{2,26},{10... | collective-permute-start | bytes 196616 | tf_op jit(solution)/shard_map/ppermute | solution.py:303
  8.9 5.6 %collective-permute-start.1 = (bf16[32,1024]{1,0:T(8,128)(2,1)S(1)}, bf16[32,1024]{1,0:T(8,128)(2,1)S(1)}, u32[]{:S(2)}, u32[]{:S(2)}) collective-permute-start(bf16[32,1024]{1,0:T(8,128)(2,1)S(1)} %get-tuple-element.31), channel_id=1, source_target_pairs={{0,16},{8,24},{16,0},{24,8},{1,17},{9,25},{17,1},{25,9},{2,18},{10... | collective-permute-start | bytes 196616 | tf_op jit(solution)/shard_map/ppermute | solution.py:303
  8.9 5.6 %collective-permute-start.2 = (bf16[32,1024]{1,0:T(8,128)(2,1)S(1)}, bf16[32,1024]{1,0:T(8,128)(2,1)S(1)}, u32[]{:S(2)}, u32[]{:S(2)}) collective-permute-start(bf16[32,1024]{1,0:T(8,128)(2,1)S(1)} %get-tuple-element.32), channel_id=1, source_target_pairs={{0,8},{8,0},{16,24},{24,16},{1,9},{9,1},{17,25},{25,17},{2,10},{10... | collective-permute-start | bytes 196616 | tf_op jit(solution)/shard_map/ppermute | solution.py:303
  14.5 7.5 %collective-permute-start.7 = (bf16[32,1024]{1,0:T(8,128)(2,1)S(1)}, bf16[32,1024]{1,0:T(8,128)(2,1)S(1)}, u32[]{:S(2)}, u32[]{:S(2)}) collective-permute-start(bf16[32,1024]{1,0:T(8,128)(2,1)S(1)} %share.1.refs_0_), channel_id=1, source_target_pairs={{0,24},{8,16},{16,8},{24,0},{1,25},{9,17},{17,9},{25,1},{2,26},{10... | collective-permute-start | bytes 196616 | tf_op jit(solution)/shard_map/ppermute | solution.py:303
  17.3 6.3 %collective-permute-start.6 = (bf16[32,1024]{1,0:T(8,128)(2,1)S(1)}, bf16[32,1024]{1,0:T(8,128)(2,1)S(1)}, u32[]{:S(2)}, u32[]{:S(2)}) collective-permute-start(bf16[32,1024]{1,0:T(8,128)(2,1)S(1)} %share.1.refs_0_), channel_id=1, source_target_pairs={{0,16},{8,24},{16,0},{24,8},{1,17},{9,25},{17,1},{25,9},{2,18},{10... | collective-permute-start | bytes 196616 | tf_op jit(solution)/shard_map/ppermute | solution.py:303
  17.3 6.3 %collective-permute-start.5 = (bf16[32,1024]{1,0:T(8,128)(2,1)S(1)}, bf16[32,1024]{1,0:T(8,128)(2,1)S(1)}, u32[]{:S(2)}, u32[]{:S(2)}) collective-permute-start(bf16[32,1024]{1,0:T(8,128)(2,1)S(1)} %share.1.refs_0_), channel_id=1, source_target_pairs={{0,8},{8,0},{16,24},{24,16},{1,9},{9,1},{17,25},{25,17},{2,10},{10... | collective-permute-start | bytes 196616 | tf_op jit(solution)/shard_map/ppermute | solution.py:303
  19.0 4.6 %collective-permute-start.4 = (bf16[32,1024]{1,0:T(8,128)(2,1)S(1)}, bf16[32,1024]{1,0:T(8,128)(2,1)S(1)}, u32[]{:S(2)}, u32[]{:S(2)}) collective-permute-start(bf16[32,1024]{1,0:T(8,128)(2,1)S(1)} %share.1.refs_0_), channel_id=1, source_target_pairs={{0,2},{1,5},{2,0},{3,7},{4,6},{5,1},{6,4},{7,3},{8,10},{9,13},{10,... | collective-permute-start | bytes 196616 | tf_op jit(solution)/shard_map/ppermute | solution.py:303
  20.5 4.3 %collective-permute-start.3 = (bf16[32,1024]{1,0:T(8,128)(2,1)S(1)}, bf16[32,1024]{1,0:T(8,128)(2,1)S(1)}, u32[]{:S(2)}, u32[]{:S(2)}) collective-permute-start(bf16[32,1024]{1,0:T(8,128)(2,1)S(1)} %share.1.refs_0_), channel_id=1, source_target_pairs={{0,4},{1,3},{2,6},{3,1},{4,0},{5,7},{6,2},{7,5},{8,12},{9,11},{10,... | collective-permute-start | bytes 196616 | tf_op jit(solution)/shard_map/ppermute | solution.py:303
  24.7 6.4 %collective-permute-start.11 = (bf16[96,1024]{1,0:T(8,128)(2,1)S(1)}, bf16[96,1024]{1,0:T(8,128)(2,1)S(1)}, u32[]{:S(2)}, u32[]{:S(2)}) collective-permute-start(bf16[96,1024]{1,0:T(8,128)(2,1)S(1)} %pad_maximum_fusion.1), channel_id=1, source_target_pairs={{0,1},{1,0},{2,3},{3,2},{4,5},{5,4},{6,7},{7,6},{8,9},{9,8},{10,11... | collective-permute-start | bytes 589832 | tf_op jit(solution)/shard_map/ppermute | solution.py:303
  24.8 6.3 %collective-permute-start.12 = (bf16[96,1024]{1,0:T(8,128)(2,1)S(1)}, bf16[96,1024]{1,0:T(8,128)(2,1)S(1)}, u32[]{:S(2)}, u32[]{:S(2)}) collective-permute-start(bf16[96,1024]{1,0:T(8,128)(2,1)S(1)} %pad_maximum_fusion.refs_1_), channel_id=1, source_target_pairs={{0,1},{1,0},{2,3},{3,2},{4,5},{5,4},{6,7},{7,6},{8,9},{9,8},{10,11... | collective-permute-start | bytes 589832 | tf_op jit(solution)/shard_map/ppermute | solution.py:303
  25.3 7.4 %collective-permute-start.9 = (bf16[96,1024]{1,0:T(8,128)(2,1)S(1)}, bf16[96,1024]{1,0:T(8,128)(2,1)S(1)}, u32[]{:S(2)}, u32[]{:S(2)}) collective-permute-start(bf16[96,1024]{1,0:T(8,128)(2,1)S(1)} %pad_maximum_fusion.refs_1_), channel_id=1, source_target_pairs={{0,4},{1,3},{2,6},{3,1},{4,0},{5,7},{6,2},{7,5},{8,12},{9,11},{10,... | collective-permute-start | bytes 589832 | tf_op jit(solution)/shard_map/ppermute | solution.py:303
  26.8 4.3 %collective-permute-start.10 = (bf16[32,1024]{1,0:T(8,128)(2,1)S(1)}, bf16[32,1024]{1,0:T(8,128)(2,1)S(1)}, u32[]{:S(2)}, u32[]{:S(2)}) collective-permute-start(bf16[32,1024]{1,0:T(8,128)(2,1)S(1)} %collective-permute-done.3.refs_2_), channel_id=1, source_target_pairs={{0,2},{1,5},{2,0},{3,7},{4,6},{5,1},{6,4},{7,3},{8,10},{9,13},{10,... | collective-permute-start | bytes 196616 | tf_op jit(solution)/shard_map/ppermute | solution.py:303
  27.4 5.9 %collective-permute-start.8 = (bf16[96,1024]{1,0:T(8,128)(2,1)S(1)}, bf16[96,1024]{1,0:T(8,128)(2,1)S(1)}, u32[]{:S(2)}, u32[]{:S(2)}) collective-permute-start(bf16[96,1024]{1,0:T(8,128)(2,1)S(1)} %pad_maximum_fusion.refs_1_), channel_id=1, source_target_pairs={{0,2},{1,5},{2,0},{3,7},{4,6},{5,1},{6,4},{7,3},{8,10},{9,13},{10,... | collective-permute-start | bytes 589832 | tf_op jit(solution)/shard_map/ppermute | solution.py:303
  32.7 5.7 %collective-permute-start.13 = (bf16[96,1024]{1,0:T(8,128)(2,1)S(1)}, bf16[96,1024]{1,0:T(8,128)(2,1)S(1)}, u32[]{:S(2)}, u32[]{:S(2)}) collective-permute-start(bf16[96,1024]{1,0:T(8,128)(2,1)S(1)} %collective-permute-done.9.refs_5_), channel_id=1, source_target_pairs={{0,2},{1,5},{2,0},{3,7},{4,6},{5,1},{6,4},{7,3},{8,10},{9,13},{10,... | collective-permute-start | bytes 589832 | tf_op jit(solution)/shard_map/ppermute | solution.py:303
  33.3 5.6 %collective-permute-start.15 = (bf16[96,1024]{1,0:T(8,128)(2,1)S(1)}, bf16[96,1024]{1,0:T(8,128)(2,1)S(1)}, u32[]{:S(2)}, u32[]{:S(2)}) collective-permute-start(bf16[96,1024]{1,0:T(8,128)(2,1)S(1)} %collective-permute-done.9.refs_5_), channel_id=1, source_target_pairs={{0,1},{1,0},{2,3},{3,2},{4,5},{5,4},{6,7},{7,6},{8,9},{9,8},{10,11... | collective-permute-start | bytes 589832 | tf_op jit(solution)/shard_map/ppermute | solution.py:303
  38.4 1.8 %collective-permute-start.16 = (bf16[96,1024]{1,0:T(8,128)(2,1)S(1)}, bf16[96,1024]{1,0:T(8,128)(2,1)S(1)}, u32[]{:S(2)}, u32[]{:S(2)}) collective-permute-start(bf16[96,1024]{1,0:T(8,128)(2,1)S(1)} %collective-permute-done.8.refs_6_), channel_id=1, source_target_pairs={{0,1},{1,0},{2,3},{3,2},{4,5},{5,4},{6,7},{7,6},{8,9},{9,8},{10,11... | collective-permute-start | bytes 589832 | tf_op jit(solution)/shard_map/ppermute | solution.py:303
  38.4 1.8 %collective-permute-start.17 = (bf16[96,1024]{1,0:T(8,128)(2,1)S(1)}, bf16[96,1024]{1,0:T(8,128)(2,1)S(1)}, u32[]{:S(2)}, u32[]{:S(2)}) collective-permute-start(bf16[96,1024]{1,0:T(8,128)(2,1)S(1)} %collective-permute-done.13.refs_7_), channel_id=1, source_target_pairs={{0,1},{1,0},{2,3},{3,2},{4,5},{5,4},{6,7},{7,6},{8,9},{9,8},{10,11... | collective-permute-start | bytes 589832 | tf_op jit(solution)/shard_map/ppermute | solution.py:303
  38.9 1.3 %collective-permute-start.14 = (bf16[32,1024]{1,0:T(8,128)(2,1)S(1)}, bf16[32,1024]{1,0:T(8,128)(2,1)S(1)}, u32[]{:S(2)}, u32[]{:S(2)}) collective-permute-start(bf16[32,1024]{1,0:T(8,128)(2,1)S(1)} %collective-permute-done.10.refs_4_), channel_id=1, source_target_pairs={{0,1},{1,0},{2,3},{3,2},{4,5},{5,4},{6,7},{7,6},{8,9},{9,8},{10,11... | collective-permute-start | bytes 196616 | tf_op jit(solution)/shard_map/ppermute | solution.py:303
  55.3 7.2 %collective-permute-start.20 = (bf16[144,256]{1,0:T(8,128)(2,1)S(1)}, bf16[144,256]{1,0:T(8,128)(2,1)S(1)}, u32[]{:S(2)}, u32[]{:S(2)}) collective-permute-start(bf16[144,256]{1,0:T(8,128)(2,1)S(1)} %sums.1.refs_0_), channel_id=1, source_target_pairs={{0,8},{8,0},{16,24},{24,16},{1,9},{9,1},{17,25},{25,17},{2,10},{10... | collective-permute-start | bytes 221192 | tf_op jit(solution)/shard_map/ppermute | solution.py:303
  55.8 8.2 %collective-permute-start.19 = (bf16[144,256]{1,0:T(8,128)(2,1)S(1)}, bf16[144,256]{1,0:T(8,128)(2,1)S(1)}, u32[]{:S(2)}, u32[]{:S(2)}) collective-permute-start(bf16[144,256]{1,0:T(8,128)(2,1)S(1)} %sums.1.refs_0_), channel_id=1, source_target_pairs={{0,16},{8,24},{16,0},{24,8},{1,17},{9,25},{17,1},{25,9},{2,18},{10... | collective-permute-start | bytes 221192 | tf_op jit(solution)/shard_map/ppermute | solution.py:303
  58.7 6.3 %collective-permute-start.18 = (bf16[144,256]{1,0:T(8,128)(2,1)S(1)}, bf16[144,256]{1,0:T(8,128)(2,1)S(1)}, u32[]{:S(2)}, u32[]{:S(2)}) collective-permute-start(bf16[144,256]{1,0:T(8,128)(2,1)S(1)} %sums.1.refs_0_), channel_id=1, source_target_pairs={{0,24},{8,16},{16,8},{24,0},{1,25},{9,17},{17,9},{25,1},{2,26},{10... | collective-permute-start | bytes 221192 | tf_op jit(solution)/shard_map/ppermute | solution.py:303
where the time goes:
time: 65.8 us; the launch traced here: 65.7 us
  Pallas kernels  23.6 us (36%)
  starting transfers between devices  22.9 us (35%)
  waiting for transfers between devices  18.3 us (28%)
  between operations  0.7 us (1%)
    ppermute x21, starting transfers between devices, swap(): lax.ppermute(value, axis, [(i, i ^ (odd_mask if i % 2 else mask)) for i i...  22.9 us
    ppermute x21, waiting for transfers between devices, swap(): lax.ppermute(value, axis, [(i, i ^ (odd_mask if i % 2 else mask)) for i i...  18.3 us
    pallas_call x1, Pallas kernels, polar(): pl.pallas_call(kernel, out_shape=jax.ShapeDtypeStruct((own, dim), bf16),...  12.2 us
    pallas_call x4, Pallas kernels, small_call(): pl.pallas_call(kernel, out_shape=jax.ShapeDtypeStruct(shape, dtype), in_s...  6.41 us
    pallas_call x1, Pallas kernels, cross_partial(): pl.pallas_call(functools.partial(cross_kernel, dp=dp), out_shape=shapes,...  3.11 us
    pallas_call x1, Pallas kernels, onehot_call(): pl.pallas_call(onehot_kernel, out_shape=(jax.ShapeDtypeStruct((subs * LOW...  1.93 us
  transfers between devices with their start and end apart: 21, of which 9 were waited for; matrix products, arithmetic and copies ran while one was open for 0% of the time, Pallas kernels for 7%

commit v1 on v0

--- a/solution.py
+++ b/solution.py
@@ -335,35 +335,27 @@
                 block = lax.dynamic_update_slice_in_dim(block, pieces[k], (place ^ k) * size, 0)
             held = [block]
         else:
-            held = [piece]
-            if dp > 1:
-                held.append(jnp.concatenate([pieces[k] for k in range(1, dp)], axis=0))
+            half = max(dp // 2, 1)
+            held = [
+                jnp.concatenate([pieces[k] for k in range(at, min(at + half, dp))], axis=0)
+                for at in range(0, dp, half)
+            ]
         strides = [1 << b for b in reversed(range(code.bit_length() - 1))]
         far, near = strides[:-1], strides[-1:]
-
-        def spread(blocks, beside=()):
+        others = []
+        for block in held:
+            have = [block]
             for even, odd in zip(far, far[::-1]):
-                new = [swap(t, "code", code, even, odd) for t in blocks]
-                if beside:
-                    new, beside = lax.optimization_barrier((new, list(beside)))
-                blocks = blocks + new
-            return blocks, list(beside)
-
-        def across(block):
-            return [swap(block, "code", code, stride) for stride in near]
-
-        if held[1:]:
-            first, _ = spread(held[:1])
-            known = 1 + len(first) // 2
-            early, rest = lax.optimization_barrier((first[:known], held[1]))
-            crossed = across(jnp.concatenate(early, axis=0)) + across(rest)
-            blocks, beside = spread([rest], first[known:] + crossed)
-            late, crossed = beside[: len(first) - known], beside[len(first) - known :]
-            held = [early[0], rest] + early[1:] + late + blocks[1:] + crossed
-            held += [t for block in late + blocks[1:] for t in across(block)]
-        else:
-            held, _ = spread(held)
-            held += [t for block in held for t in across(block)]
+                send = have[0] if len(have) == 1 else jnp.concatenate(have, axis=0)
+                have.append(swap(send, "code", code, even, odd))
+            for stride in near:
+                early = have[:-1] or have
+                crossed = [swap(jnp.concatenate(early, axis=0), "code", code, stride)]
+                if have[1:]:
+                    crossed.append(swap(have[-1], "code", code, stride))
+                have += crossed
+            others += have[1:]
+        held += others
         rotation_t = polar(held, own, 1 if thin else dp)
         scratch = [pltpu.VMEM((own, words), f32)]
         operands = (rotation_t, res_v, codes_v, onehot, counts)

time: 65.8 us -> 63.5 us (0.965)
  starting transfers between devices: 22.9 us -> 19.1 us
  waiting for transfers between devices: 18.3 us -> 19.8 us
    ppermute x21 -> x17, starting transfers between devices: 22.9 us -> 19.1 us  [swap(): lax.ppermute(value, axis, [(i, i ^ (odd_mask if i % 2 else mask)) for i i...]
    ppermute x21 -> x17, waiting for transfers between devices: 18.3 us -> 19.8 us  [swap(): lax.ppermute(value, axis, [(i, i ^ (odd_mask if i % 2 else mask)) for i i...]
  transfers between devices with their start and end apart: 21 -> 17, of which waited for: 9 -> 8; matrix products, arithmetic and copies ran while one was open for 0% -> 0% of each run, Pallas kernels for 7% -> 7%
where the time goes in v1:
time: 63.5 us; the launch traced here: 63.4 us
  Pallas kernels  23.6 us (37%)
  waiting for transfers between devices  19.8 us (31%)
  starting transfers between devices  19.1 us (30%)
  between operations  0.72 us (1%)
    ppermute x17, waiting for transfers between devices, swap(): lax.ppermute(value, axis, [(i, i ^ (odd_mask if i % 2 else mask)) for i i...  19.8 us
    ppermute x17, starting transfers between devices, swap(): lax.ppermute(value, axis, [(i, i ^ (odd_mask if i % 2 else mask)) for i i...  19.1 us
    pallas_call x1, Pallas kernels, polar(): pl.pallas_call(kernel, out_shape=jax.ShapeDtypeStruct((own, dim), bf16),...  12.2 us
    pallas_call x4, Pallas kernels, small_call(): pl.pallas_call(kernel, out_shape=jax.ShapeDtypeStruct(shape, dtype), in_s...  6.42 us
    pallas_call x1, Pallas kernels, cross_partial(): pl.pallas_call(functools.partial(cross_kernel, dp=dp), out_shape=shapes,...  3.11 us
    pallas_call x1, Pallas kernels, onehot_call(): pl.pallas_call(onehot_kernel, out_shape=(jax.ShapeDtypeStruct((subs * LOW...  1.93 us
  transfers between devices with their start and end apart: 17, of which 8 were waited for; matrix products, arithmetic and copies ran while one was open for 0% of the time, Pallas kernels for 7%

profile of v1, /device:TPU:0, one launch (start us, length us, event | category | flops | bytes accessed | tf_op | source)
XLA Modules:
  0.0 63.4 jit_solution(308949721520561613)
XLA Ops:
  0.6 3.1 %cross_partial.1 = (f32[32,1024]{1,0:T(8,128)S(1)}, bf16[32,1024]{1,0:T(8,128)(2,1)S(1)}, bf16[32,1024]{1,0:T(8,128)(2,1)S(1)}, bf16[32,1024]{1,0:T(8,128)(2,1)S...) custom-call(s32[16,2048]{1,0:T(8,128)} %bitcast.7, f32[128,256]{1,0:T(8,128)} %bitcast.8, ...), custom_call_target="tpu_custom_call" | custom-call | tf_op jit(solution)/shard_map/cross_partial/pallas_call | solution.py:78
  3.7 5.1 %collective-permute-start = (bf16[32,1024]{1,0:T(8,128)(2,1)S(1)}, bf16[32,1024]{1,0:T(8,128)(2,1)S(1)}, u32[]{:S(2)}, u32[]{:S(2)}) collective-permute-start(bf16[32,1024]{1,0:T(8,128)(2,1)S(1)} %get-tuple-element.17), channel_id=1, source_target_pairs={{0,24},{8,16},{16,8},{24,0},{1,25},{9,17},{17,9},{25,1},{2,26},{10... | collective-permute-start | bytes 196616 | tf_op jit(solution)/shard_map/ppermute | solution.py:303
  8.9 0.0 collective-permute-start.1
  8.9 0.6 %collective-permute-start.2 = (bf16[32,1024]{1,0:T(8,128)(2,1)S(1)}, bf16[32,1024]{1,0:T(8,128)(2,1)S(1)}, u32[]{:S(2)}, u32[]{:S(2)}) collective-permute-start(bf16[32,1024]{1,0:T(8,128)(2,1)S(1)} %get-tuple-element.19), channel_id=1, source_target_pairs={{0,8},{8,0},{16,24},{24,16},{1,9},{9,1},{17,25},{25,17},{2,10},{10... | collective-permute-start | bytes 196616 | tf_op jit(solution)/shard_map/ppermute | solution.py:303
  9.5 1.9 %onehot.1 = (bf16[1024,2048]{1,0:T(8,128)(2,1)S(1)}, f32[16,256]{1,0:T(8,128)S(1)}) custom-call(s32[16,2048]{1,0:T(8,128)S(1)} %get-tuple-element.20.codes_ref), custom_call_target="tpu_custom_call" | custom-call | flops 1073741824 | bytes 4194304 | tf_op jit(solution)/shard_map/onehot/pallas_call | solution.py:192
  11.4 0.0 collective-permute-done.refs_1_
  11.5 3.0 %collective-permute-done.1.refs_2_ = bf16[32,1024]{1,0:T(8,128)(2,1)S(1)} collective-permute-done((bf16[32,1024]{1,0:T(8,128)(2,1)S(1)}, bf16[32,1024]{1,0:T(8,128)(2,1)S(1)}, u32[]{:S(2)}, u32[]{:S(2)}) %collective-permute-start.1) | collective-permute-done | bytes 65568 | tf_op jit(solution)/shard_map/ppermute | solution.py:303
  14.5 0.0 collective-permute-done.2.refs_3_
  14.5 1.1 %collective-permute-start.3 = (bf16[32,1024]{1,0:T(8,128)(2,1)S(1)}, bf16[32,1024]{1,0:T(8,128)(2,1)S(1)}, u32[]{:S(2)}, u32[]{:S(2)}) collective-permute-start(bf16[32,1024]{1,0:T(8,128)(2,1)S(1)} %share.1), channel_id=1, source_target_pairs={{0,8},{8,0},{16,24},{24,16},{1,9},{9,1},{17,25},{25,17},{2,10},{10... | collective-permute-start | bytes 196616 | tf_op jit(solution)/shard_map/ppermute | solution.py:303
  15.7 2.0 %collective-permute-start.5 = (bf16[32,1024]{1,0:T(8,128)(2,1)S(1)}, bf16[32,1024]{1,0:T(8,128)(2,1)S(1)}, u32[]{:S(2)}, u32[]{:S(2)}) collective-permute-start(bf16[32,1024]{1,0:T(8,128)(2,1)S(1)} %share.1), channel_id=1, source_target_pairs={{0,24},{8,16},{16,8},{24,0},{1,25},{9,17},{17,9},{25,1},{2,26},{10... | collective-permute-start | bytes 196616 | tf_op jit(solution)/shard_map/ppermute | solution.py:303
  17.6 0.4 collective-permute-start.4
  18.1 1.8 %collective-permute-done.3 = bf16[32,1024]{1,0:T(8,128)(2,1)S(1)} collective-permute-done((bf16[32,1024]{1,0:T(8,128)(2,1)S(1)}, bf16[32,1024]{1,0:T(8,128)(2,1)S(1)}, u32[]{:S(2)}, u32[]{:S(2)}) %collective-permute-start.3) | collective-permute-done | bytes 65568 | tf_op jit(solution)/shard_map/ppermute | solution.py:303
  19.9 0.6 collective-permute-start.6
  20.4 3.2 %collective-permute-done.4 = bf16[32,1024]{1,0:T(8,128)(2,1)S(1)} collective-permute-done((bf16[32,1024]{1,0:T(8,128)(2,1)S(1)}, bf16[32,1024]{1,0:T(8,128)(2,1)S(1)}, u32[]{:S(2)}, u32[]{:S(2)}) %collective-permute-start.4) | collective-permute-done | bytes 65568 | tf_op jit(solution)/shard_map/ppermute | solution.py:303
  23.7 0.0 collective-permute-done.5
  23.7 1.8 %collective-permute-start.10 = (bf16[64,1024]{1,0:T(8,128)(2,1)S(1)}, bf16[64,1024]{1,0:T(8,128)(2,1)S(1)}, u32[]{:S(2)}, u32[]{:S(2)}) collective-permute-start(bf16[64,1024]{1,0:T(8,128)(2,1)S(1)} %get-tuple-element.31.refs_1_), channel_id=1, source_target_pairs={{0,4},{1,3},{2,6},{3,1},{4,0},{5,7},{6,2},{7,5},{8,12},{9,11},{10,... | collective-permute-start | bytes 393224 | tf_op jit(solution)/shard_map/ppermute | solution.py:303
  25.5 0.0 collective-permute-done.6.refs_2_
  25.5 1.6 %collective-permute-start.7 = (bf16[128,1024]{1,0:T(8,128)(2,1)S(1)}, bf16[128,1024]{1,0:T(8,128)(2,1)S(1)}, u32[]{:S(2)}, u32[]{:S(2)}) collective-permute-start(bf16[128,1024]{1,0:T(8,128)(2,1)S(1)} %pad_maximum_fusion), channel_id=1, source_target_pairs={{0,2},{1,5},{2,0},{3,7},{4,6},{5,1},{6,4},{7,3},{8,10},{9,13},{10,... | collective-permute-start | bytes 786440 | tf_op jit(solution)/shard_map/ppermute | solution.py:303
  27.0 3.1 %collective-permute-done.10.refs_6_ = bf16[64,1024]{1,0:T(8,128)(2,1)S(1)} collective-permute-done((bf16[64,1024]{1,0:T(8,128)(2,1)S(1)}, bf16[64,1024]{1,0:T(8,128)(2,1)S(1)}, u32[]{:S(2)}, u32[]{:S(2)}) %collective-permute-start.10) | collective-permute-done | bytes 131104 | tf_op jit(solution)/shard_map/ppermute | solution.py:303
  30.2 0.9 %collective-permute-start.11 = (bf16[128,1024]{1,0:T(8,128)(2,1)S(1)}, bf16[128,1024]{1,0:T(8,128)(2,1)S(1)}, u32[]{:S(2)}, u32[]{:S(2)}) collective-permute-start(bf16[128,1024]{1,0:T(8,128)(2,1)S(1)} %constant_dynamic-update-slice_fusion.2), channel_id=1, source_target_pairs={{0,2},{1,5},{2,0},{3,7},{4,6},{5,1},{6,4},{7,3},{8,10},{9,13},{10,... | collective-permute-start | bytes 786440 | tf_op jit(solution)/shard_map/ppermute | solution.py:303
  31.1 0.0 collective-permute-start.8
  31.1 0.5 collective-permute-start.12
  31.6 0.3 collective-permute-done.7.refs_3_
  31.9 0.0 collective-permute-start.9
  31.9 4.7 %collective-permute-done.11.refs_7_ = bf16[128,1024]{1,0:T(8,128)(2,1)S(1)} collective-permute-done((bf16[128,1024]{1,0:T(8,128)(2,1)S(1)}, bf16[128,1024]{1,0:T(8,128)(2,1)S(1)}, u32[]{:S(2)}, u32[]{:S(2)}) %collective-permute-start.11) | collective-permute-done | bytes 262176 | tf_op jit(solution)/shard_map/ppermute | solution.py:303
  36.6 0.0 collective-permute-start.13
  36.6 0.0 collective-permute-done.8.refs_4_
  36.6 0.0 collective-permute-done.12.refs_8_
  36.6 0.0 collective-permute-done.9.refs_5_
  36.6 1.5 %collective-permute-done.13.refs_9_ = bf16[128,1024]{1,0:T(8,128)(2,1)S(1)} collective-permute-done((bf16[128,1024]{1,0:T(8,128)(2,1)S(1)}, bf16[128,1024]{1,0:T(8,128)(2,1)S(1)}, u32[]{:S(2)}, u32[]{:S(2)}) %collective-permute-start.13) | collective-permute-done | bytes 262176 | tf_op jit(solution)/shard_map/ppermute | solution.py:303
  38.1 12.2 %polar.1.rot_ref = bf16[128,1024]{1,0:T(8,128)(2,1)S(1)} custom-call(bf16[64,1024]{1,0:T(8,128)(2,1)S(1)} %pad_maximum_fusion.1.refs_0_, bf16[64,1024]{1,0:T(8,128)(2,1)S(1)} %get-tuple-element.31.refs_1_, bf16[64,1024]{1,0:T(8,128)(2,1)S(1)} %collective-permute-done.6.refs_2_, bf16[128,1024]{1,0:T(8,128)(2,1)S(1)} %collective-permute-done.7.refs_3_, ...), custom_call_target="tpu_custom_call" | custom-call | tf_op jit(solution)/shard_map/polar/pallas_call | solution.py:248
  50.3 3.0 %sums.1.refs_0_ = bf16[144,256]{1,0:T(8,128)(2,1)S(1)} custom-call(bf16[128,1024]{1,0:T(8,128)(2,1)S(1)} %polar.1.rot_ref, bf16[2048,1024]{1,0:T(8,128)(2,1)S(1)} %get-tuple-element.26.res_ref, s32[16,2048]{1,0:T(8,128)S(1)} %get-tuple-element.20.codes_ref, bf16[1024,2048]{1,0:T(8,128)(2,1)S(1)} %get-tuple-element.28.onehot_ref, ...), custom_call_target="tpu_custom_call" | custom-call | tf_op jit(solution)/shard_map/sums/pallas_call | solution.py:290
  53.3 0.1 collective-permute-start.16
  53.5 2.3 %collective-permute-start.15 = (bf16[144,256]{1,0:T(8,128)(2,1)S(1)}, bf16[144,256]{1,0:T(8,128)(2,1)S(1)}, u32[]{:S(2)}, u32[]{:S(2)}) collective-permute-start(bf16[144,256]{1,0:T(8,128)(2,1)S(1)} %sums.1.refs_0_), channel_id=1, source_target_pairs={{0,16},{8,24},{16,0},{24,8},{1,17},{9,25},{17,1},{25,9},{2,18},{10... | collective-permute-start | bytes 221192 | tf_op jit(solution)/shard_map/ppermute | solution.py:303
  55.8 2.0 %collective-permute-start.14 = (bf16[144,256]{1,0:T(8,128)(2,1)S(1)}, bf16[144,256]{1,0:T(8,128)(2,1)S(1)}, u32[]{:S(2)}, u32[]{:S(2)}) collective-permute-start(bf16[144,256]{1,0:T(8,128)(2,1)S(1)} %sums.1.refs_0_), channel_id=1, source_target_pairs={{0,24},{8,16},{16,8},{24,0},{1,25},{9,17},{17,9},{25,1},{2,26},{10... | collective-permute-start | bytes 221192 | tf_op jit(solution)/shard_map/ppermute | solution.py:303
  57.8 2.7 %rotated.1 = f32[2048,128]{1,0:T(8,128)} custom-call(bf16[128,1024]{1,0:T(8,128)(2,1)S(1)} %polar.1.rot_ref, bf16[2048,1024]{1,0:T(8,128)(2,1)S(1)} %get-tuple-element.26.res_ref), custom_call_target="tpu_custom_call" | custom-call | tf_op jit(solution)/shard_map/rotated/pallas_call | solution.py:290
  60.5 0.0 collective-permute-done.16.refs_3_
  60.5 2.2 %collective-permute-done.15.refs_2_ = bf16[144,256]{1,0:T(8,128)(2,1)S(1)} collective-permute-done((bf16[144,256]{1,0:T(8,128)(2,1)S(1)}, bf16[144,256]{1,0:T(8,128)(2,1)S(1)}, u32[]{:S(2)}, u32[]{:S(2)}) %collective-permute-start.15) | collective-permute-done | bytes 73760 | tf_op jit(solution)/shard_map/ppermute | solution.py:303
  62.6 0.0 collective-permute-done.14.refs_1_
  62.6 0.7 %book.1 = f32[128,256]{1,0:T(8,128)} custom-call(f32[128,256]{1,0:T(8,128)S(1)} %get-tuple-element.27.book_ref, bf16[144,256]{1,0:T(8,128)(2,1)S(1)} %sums.1.refs_0_, bf16[144,256]{1,0:T(8,128)(2,1)S(1)} %collective-permute-done.14.refs_1_, bf16[144,256]{1,0:T(8,128)(2,1)S(1)} %collective-permute-done.15.refs_2_, ...), custom_call_target="tpu_custom_call" | custom-call | tf_op jit(solution)/shard_map/book/pallas_call | solution.py:290
  (6 shorter events, 0.1 us)
Async XLA Ops:
  3.7 7.7 %collective-permute-start = (bf16[32,1024]{1,0:T(8,128)(2,1)S(1)}, bf16[32,1024]{1,0:T(8,128)(2,1)S(1)}, u32[]{:S(2)}, u32[]{:S(2)}) collective-permute-start(bf16[32,1024]{1,0:T(8,128)(2,1)S(1)} %get-tuple-element.17), channel_id=1, source_target_pairs={{0,24},{8,16},{16,8},{24,0},{1,25},{9,17},{17,9},{25,1},{2,26},{10... | collective-permute-start | bytes 196616 | tf_op jit(solution)/shard_map/ppermute | solution.py:303
  8.9 5.6 %collective-permute-start.1 = (bf16[32,1024]{1,0:T(8,128)(2,1)S(1)}, bf16[32,1024]{1,0:T(8,128)(2,1)S(1)}, u32[]{:S(2)}, u32[]{:S(2)}) collective-permute-start(bf16[32,1024]{1,0:T(8,128)(2,1)S(1)} %get-tuple-element.18), channel_id=1, source_target_pairs={{0,16},{8,24},{16,0},{24,8},{1,17},{9,25},{17,1},{25,9},{2,18},{10... | collective-permute-start | bytes 196616 | tf_op jit(solution)/shard_map/ppermute | solution.py:303
  8.9 5.6 %collective-permute-start.2 = (bf16[32,1024]{1,0:T(8,128)(2,1)S(1)}, bf16[32,1024]{1,0:T(8,128)(2,1)S(1)}, u32[]{:S(2)}, u32[]{:S(2)}) collective-permute-start(bf16[32,1024]{1,0:T(8,128)(2,1)S(1)} %get-tuple-element.19), channel_id=1, source_target_pairs={{0,8},{8,0},{16,24},{24,16},{1,9},{9,1},{17,25},{25,17},{2,10},{10... | collective-permute-start | bytes 196616 | tf_op jit(solution)/shard_map/ppermute | solution.py:303
  14.5 5.3 %collective-permute-start.3 = (bf16[32,1024]{1,0:T(8,128)(2,1)S(1)}, bf16[32,1024]{1,0:T(8,128)(2,1)S(1)}, u32[]{:S(2)}, u32[]{:S(2)}) collective-permute-start(bf16[32,1024]{1,0:T(8,128)(2,1)S(1)} %share.1), channel_id=1, source_target_pairs={{0,8},{8,0},{16,24},{24,16},{1,9},{9,1},{17,25},{25,17},{2,10},{10... | collective-permute-start | bytes 196616 | tf_op jit(solution)/shard_map/ppermute | solution.py:303
  15.7 8.0 %collective-permute-start.5 = (bf16[32,1024]{1,0:T(8,128)(2,1)S(1)}, bf16[32,1024]{1,0:T(8,128)(2,1)S(1)}, u32[]{:S(2)}, u32[]{:S(2)}) collective-permute-start(bf16[32,1024]{1,0:T(8,128)(2,1)S(1)} %share.1), channel_id=1, source_target_pairs={{0,24},{8,16},{16,8},{24,0},{1,25},{9,17},{17,9},{25,1},{2,26},{10... | collective-permute-start | bytes 196616 | tf_op jit(solution)/shard_map/ppermute | solution.py:303
  17.6 6.0 %collective-permute-start.4 = (bf16[32,1024]{1,0:T(8,128)(2,1)S(1)}, bf16[32,1024]{1,0:T(8,128)(2,1)S(1)}, u32[]{:S(2)}, u32[]{:S(2)}) collective-permute-start(bf16[32,1024]{1,0:T(8,128)(2,1)S(1)} %share.1), channel_id=1, source_target_pairs={{0,16},{8,24},{16,0},{24,8},{1,17},{9,25},{17,1},{25,9},{2,18},{10... | collective-permute-start | bytes 196616 | tf_op jit(solution)/shard_map/ppermute | solution.py:303
  19.9 5.6 %collective-permute-start.6 = (bf16[64,1024]{1,0:T(8,128)(2,1)S(1)}, bf16[64,1024]{1,0:T(8,128)(2,1)S(1)}, u32[]{:S(2)}, u32[]{:S(2)}) collective-permute-start(bf16[64,1024]{1,0:T(8,128)(2,1)S(1)} %pad_maximum_fusion.1.refs_0_), channel_id=1, source_target_pairs={{0,4},{1,3},{2,6},{3,1},{4,0},{5,7},{6,2},{7,5},{8,12},{9,11},{10,... | collective-permute-start | bytes 393224 | tf_op jit(solution)/shard_map/ppermute | solution.py:303
  23.7 6.5 %collective-permute-start.10 = (bf16[64,1024]{1,0:T(8,128)(2,1)S(1)}, bf16[64,1024]{1,0:T(8,128)(2,1)S(1)}, u32[]{:S(2)}, u32[]{:S(2)}) collective-permute-start(bf16[64,1024]{1,0:T(8,128)(2,1)S(1)} %get-tuple-element.31.refs_1_), channel_id=1, source_target_pairs={{0,4},{1,3},{2,6},{3,1},{4,0},{5,7},{6,2},{7,5},{8,12},{9,11},{10,... | collective-permute-start | bytes 393224 | tf_op jit(solution)/shard_map/ppermute | solution.py:303
  25.5 6.4 %collective-permute-start.7 = (bf16[128,1024]{1,0:T(8,128)(2,1)S(1)}, bf16[128,1024]{1,0:T(8,128)(2,1)S(1)}, u32[]{:S(2)}, u32[]{:S(2)}) collective-permute-start(bf16[128,1024]{1,0:T(8,128)(2,1)S(1)} %pad_maximum_fusion), channel_id=1, source_target_pairs={{0,2},{1,5},{2,0},{3,7},{4,6},{5,1},{6,4},{7,3},{8,10},{9,13},{10,... | collective-permute-start | bytes 786440 | tf_op jit(solution)/shard_map/ppermute | solution.py:303
  30.2 6.4 %collective-permute-start.11 = (bf16[128,1024]{1,0:T(8,128)(2,1)S(1)}, bf16[128,1024]{1,0:T(8,128)(2,1)S(1)}, u32[]{:S(2)}, u32[]{:S(2)}) collective-permute-start(bf16[128,1024]{1,0:T(8,128)(2,1)S(1)} %constant_dynamic-update-slice_fusion.2), channel_id=1, source_target_pairs={{0,2},{1,5},{2,0},{3,7},{4,6},{5,1},{6,4},{7,3},{8,10},{9,13},{10,... | collective-permute-start | bytes 786440 | tf_op jit(solution)/shard_map/ppermute | solution.py:303
  31.1 5.5 %collective-permute-start.8 = (bf16[128,1024]{1,0:T(8,128)(2,1)S(1)}, bf16[128,1024]{1,0:T(8,128)(2,1)S(1)}, u32[]{:S(2)}, u32[]{:S(2)}) collective-permute-start(bf16[128,1024]{1,0:T(8,128)(2,1)S(1)} %pad_maximum_fusion), channel_id=1, source_target_pairs={{0,1},{1,0},{2,3},{3,2},{4,5},{5,4},{6,7},{7,6},{8,9},{9,8},{10,11... | collective-permute-start | bytes 786440 | tf_op jit(solution)/shard_map/ppermute | solution.py:303
  31.1 5.5 %collective-permute-start.12 = (bf16[128,1024]{1,0:T(8,128)(2,1)S(1)}, bf16[128,1024]{1,0:T(8,128)(2,1)S(1)}, u32[]{:S(2)}, u32[]{:S(2)}) collective-permute-start(bf16[128,1024]{1,0:T(8,128)(2,1)S(1)} %constant_dynamic-update-slice_fusion.2), channel_id=1, source_target_pairs={{0,1},{1,0},{2,3},{3,2},{4,5},{5,4},{6,7},{7,6},{8,9},{9,8},{10,11... | collective-permute-start | bytes 786440 | tf_op jit(solution)/shard_map/ppermute | solution.py:303
  31.9 4.7 %collective-permute-start.9 = (bf16[128,1024]{1,0:T(8,128)(2,1)S(1)}, bf16[128,1024]{1,0:T(8,128)(2,1)S(1)}, u32[]{:S(2)}, u32[]{:S(2)}) collective-permute-start(bf16[128,1024]{1,0:T(8,128)(2,1)S(1)} %collective-permute-done.7.refs_3_), channel_id=1, source_target_pairs={{0,1},{1,0},{2,3},{3,2},{4,5},{5,4},{6,7},{7,6},{8,9},{9,8},{10,11... | collective-permute-start | bytes 786440 | tf_op jit(solution)/shard_map/ppermute | solution.py:303
  36.6 1.5 %collective-permute-start.13 = (bf16[128,1024]{1,0:T(8,128)(2,1)S(1)}, bf16[128,1024]{1,0:T(8,128)(2,1)S(1)}, u32[]{:S(2)}, u32[]{:S(2)}) collective-permute-start(bf16[128,1024]{1,0:T(8,128)(2,1)S(1)} %collective-permute-done.11.refs_7_), channel_id=1, source_target_pairs={{0,1},{1,0},{2,3},{3,2},{4,5},{5,4},{6,7},{7,6},{8,9},{9,8},{10,11... | collective-permute-start | bytes 786440 | tf_op jit(solution)/shard_map/ppermute | solution.py:303
  53.3 7.2 %collective-permute-start.16 = (bf16[144,256]{1,0:T(8,128)(2,1)S(1)}, bf16[144,256]{1,0:T(8,128)(2,1)S(1)}, u32[]{:S(2)}, u32[]{:S(2)}) collective-permute-start(bf16[144,256]{1,0:T(8,128)(2,1)S(1)} %sums.1.refs_0_), channel_id=1, source_target_pairs={{0,8},{8,0},{16,24},{24,16},{1,9},{9,1},{17,25},{25,17},{2,10},{10... | collective-permute-start | bytes 221192 | tf_op jit(solution)/shard_map/ppermute | solution.py:303
  53.5 9.2 %collective-permute-start.15 = (bf16[144,256]{1,0:T(8,128)(2,1)S(1)}, bf16[144,256]{1,0:T(8,128)(2,1)S(1)}, u32[]{:S(2)}, u32[]{:S(2)}) collective-permute-start(bf16[144,256]{1,0:T(8,128)(2,1)S(1)} %sums.1.refs_0_), channel_id=1, source_target_pairs={{0,16},{8,24},{16,0},{24,8},{1,17},{9,25},{17,1},{25,9},{2,18},{10... | collective-permute-start | bytes 221192 | tf_op jit(solution)/shard_map/ppermute | solution.py:303
  55.8 6.8 %collective-permute-start.14 = (bf16[144,256]{1,0:T(8,128)(2,1)S(1)}, bf16[144,256]{1,0:T(8,128)(2,1)S(1)}, u32[]{:S(2)}, u32[]{:S(2)}) collective-permute-start(bf16[144,256]{1,0:T(8,128)(2,1)S(1)} %sums.1.refs_0_), channel_id=1, source_target_pairs={{0,24},{8,16},{16,8},{24,0},{1,25},{9,17},{17,9},{25,1},{2,26},{10... | collective-permute-start | bytes 221192 | tf_op jit(solution)/shard_map/ppermute | solution.py:303
